TPU v7x, 128 devices: a whole 4x4x4 slice. The times are simulated.
128 devices in a mesh: table: 8 (over y, core), seq: 16 (over z, x).
Axes of the slice: x: 4, y: 4, z: 4, core: 2. Of those that a mesh axis runs over, the one named last changes fastest.
Arguments:
- item_ids: int32 [8, 4096], P('table', 'seq'), may hold values from 0 to 524287, as said below
- history_len: int32 [8], P('table'), may hold values from 1024 to 4096, as said below
- row_place: int32 [524288], replicated, may hold values from 0 to 524287, as said below
- item_table: bfloat16 [524288, 512], P(('table', 'seq')), may hold values from -6 to 6
- input_proj: bfloat16 [512, 2048], replicated, may hold values from -0.25 to 0.25
- output_proj: bfloat16 [512, 512], replicated, may hold values from -0.25 to 0.25
- out_cotangent: bfloat16 [8, 4096, 512], P('table', 'seq'), may hold values from -18 to 18
Outputs:
- layer_out: bfloat16 [8, 4096, 512], P('table', 'seq')
- table_grad: bfloat16 [524288, 512], P(('table', 'seq'))
Inputs may be any that keep to these rules, and one draw needn't show every extreme that they name: `item_ids`: within the 256 positions of one device, at most 6 items are stored in any one owner's block of 4096 table rows (rows o * 4096 to (o + 1) * 4096 - 1); one owner's block receives exactly 6 from the positions of every device. `row_place`: A permutation: every table row holds exactly one item. `history_len`: at least one history fills all 4096 positions.
All inputs are finite; a program needn't handle non-finite values.
Results may differ from a plain program's by a relative error of at most 0.006.
Values may be sent and summed in bfloat16 or wider, within the bound.
A program may use at most 128 MiB of HBM per device.

v0:
```python
import math
import jax
import jax.numpy as jnp
from jax import lax
from jax.sharding import PartitionSpec as P

HEADS = 8
eps_norm = 1e-05
block_limit = 512


def dsilu(inputs):
    sigmoid_part = jax.nn.sigmoid(inputs)
    return sigmoid_part * (1.0 + inputs * (1.0 - sigmoid_part))


def normalize(inputs):
    centred = inputs - jnp.mean(inputs, axis=-1, keepdims=True)
    spread = jnp.sqrt(jnp.mean(centred * centred, axis=-1, keepdims=True) + eps_norm)
    return (centred / spread, spread)


def norm_back(gradient, normed, spread):
    mean_grad = jnp.mean(gradient, axis=-1, keepdims=True)
    mean_prod = jnp.mean(gradient * normed, axis=-1, keepdims=True)
    return (gradient - mean_grad - normed * mean_prod) / spread


def heads_view(matrix):
    return matrix.reshape(matrix.shape[0], HEADS, matrix.shape[1] // HEADS)


def tile_mask(query_pos, key_pos, length_user):
    return (key_pos[None, :] <= query_pos[:, None]) & (query_pos[:, None] < length_user)


def tile_forward(queries, keys_blk, values_blk, allowed, score_scale):
    scores = (
        jnp.einsum(
            "lhe,nhe->hln",
            heads_view(queries),
            heads_view(keys_blk),
            preferred_element_type=jnp.float32,
        )
        * score_scale
    )
    weights = jnp.where(allowed[None], jax.nn.silu(scores), 0.0).astype(jnp.bfloat16)
    result = jnp.einsum(
        "hln,nhe->lhe", weights, heads_view(values_blk), preferred_element_type=jnp.float32
    )
    return result.reshape(queries.shape[0], -1)


def tile_query_grad(queries, grad_rows, keys_blk, values_blk, allowed, score_scale):
    scores = (
        jnp.einsum(
            "lhe,nhe->hln",
            heads_view(queries),
            heads_view(keys_blk),
            preferred_element_type=jnp.float32,
        )
        * score_scale
    )
    weight_grad = jnp.einsum(
        "lhe,nhe->hln",
        heads_view(grad_rows),
        heads_view(values_blk),
        preferred_element_type=jnp.float32,
    )
    score_grad = jnp.where(allowed[None], weight_grad * dsilu(scores), 0.0).astype(jnp.bfloat16)
    result = jnp.einsum(
        "hln,nhe->lhe", score_grad, heads_view(keys_blk), preferred_element_type=jnp.float32
    )
    return result.reshape(queries.shape[0], -1) * score_scale


def tile_key_grad(query_piece, grad_piece, keys_mine, values_mine, allowed, score_scale):
    scores = (
        jnp.einsum(
            "lhe,nhe->hln",
            heads_view(query_piece),
            heads_view(keys_mine),
            preferred_element_type=jnp.float32,
        )
        * score_scale
    )
    weights = jnp.where(allowed[None], jax.nn.silu(scores), 0.0).astype(jnp.bfloat16)
    weight_grad = jnp.einsum(
        "lhe,nhe->hln",
        heads_view(grad_piece),
        heads_view(values_mine),
        preferred_element_type=jnp.float32,
    )
    score_grad = jnp.where(allowed[None], weight_grad * dsilu(scores), 0.0).astype(jnp.bfloat16)
    value_part = jnp.einsum(
        "hln,lhe->nhe", weights, heads_view(grad_piece), preferred_element_type=jnp.float32
    )
    key_part = jnp.einsum(
        "hln,lhe->nhe", score_grad, heads_view(query_piece), preferred_element_type=jnp.float32
    )
    key_count = keys_mine.shape[0]
    return (key_part.reshape(key_count, -1) * score_scale, value_part.reshape(key_count, -1))


def over_blocks(tile_fn, running, pieces):
    rows_in = pieces[0].shape[0]
    block_rows = math.gcd(rows_in, block_limit)
    block_count = rows_in // block_rows
    stacked = tuple(
        (member.reshape((block_count, block_rows) + member.shape[1:]) for member in pieces)
    )
    offsets = jnp.arange(block_count, dtype=jnp.int32) * block_rows

    def step_block(carried, scan_item):
        offset, blocks_now = scan_item
        return (tile_fn(carried, blocks_now, offset), None)

    result, unused = lax.scan(step_block, running, (offsets, stacked))
    return result


def local(item_ids, history_len, row_place, item_table, input_proj, output_proj, out_cotangent):
    ids_local = item_ids[0]
    length_user = history_len[0]
    seq_len = ids_local.shape[0]
    rows_dev = item_table.shape[0]
    model_width = item_table.shape[1]
    score_scale = (model_width // HEADS) ** (-0.5)
    table_count = lax.axis_size("table")
    seq_count = lax.axis_size("seq")
    owners = table_count * seq_count
    capacity = 3 * seq_len // owners
    query_first = lax.axis_index("seq") * seq_len
    positions = query_first + jnp.arange(seq_len, dtype=jnp.int32)
    live_rows = (positions < length_user).astype(jnp.float32)[:, None]
    stored = row_place[ids_local]
    owner_of = stored // rows_dev
    local_row = stored % rows_dev
    owner_hits = (owner_of[:, None] == jnp.arange(owners, dtype=jnp.int32)[None, :]).astype(
        jnp.int32
    )
    slot_rank = jnp.sum((jnp.cumsum(owner_hits, axis=0) - owner_hits) * owner_hits, axis=1)
    slot_of = owner_of * capacity + slot_rank
    requests = jnp.full((owners * capacity,), -1, jnp.int32).at[slot_of].set(local_row)
    wanted = lax.all_to_all(
        requests.reshape(owners, capacity),
        ("table", "seq"),
        split_axis=0,
        concat_axis=0,
        tiled=True,
    )
    safe_rows = jnp.maximum(wanted, 0)
    returned = lax.all_to_all(
        jnp.where((wanted >= 0)[..., None], item_table[safe_rows], 0.0),
        ("table", "seq"),
        split_axis=0,
        concat_axis=0,
        tiled=True,
    )
    answered = returned
    asked_rows = wanted
    answered = answered.reshape(owners * capacity, model_width)
    asked_rows = asked_rows.reshape(owners * capacity)
    embedded = answered[slot_of]
    normed_exact, input_spread = normalize(embedded.astype(jnp.float32))
    normed = normed_exact.astype(jnp.bfloat16)
    pre_act = jnp.dot(normed, input_proj, preferred_element_type=jnp.float32)
    activated = jax.nn.silu(pre_act)
    gate_u = activated[:, :model_width]
    values_loc = activated[:, model_width : 2 * model_width].astype(jnp.bfloat16)
    queries_loc = activated[:, 2 * model_width : 3 * model_width].astype(jnp.bfloat16)
    keys_loc = activated[:, 3 * model_width :].astype(jnp.bfloat16)
    zero_rows = jnp.zeros((seq_len, model_width), jnp.float32)

    def forward_tile(running, pieces_blk, key_start):
        keys_blk, values_blk = pieces_blk
        key_pos = key_start + jnp.arange(keys_blk.shape[0], dtype=jnp.int32)
        allowed = tile_mask(positions, key_pos, length_user)
        return running + tile_forward(queries_loc, keys_blk, values_blk, allowed, score_scale)

    attention = over_blocks(
        forward_tile,
        zero_rows,
        (
            lax.all_gather(keys_loc, "seq", axis=0, tiled=True),
            lax.all_gather(values_loc, "seq", axis=0, tiled=True),
        ),
    )
    attn_normed, attn_spread = normalize(attention)
    mixed = (attn_normed * gate_u).astype(jnp.bfloat16)
    branch = jnp.dot(mixed, output_proj, preferred_element_type=jnp.float32)
    layer_out = (live_rows * (embedded.astype(jnp.float32) + branch)).astype(jnp.bfloat16)
    cot_masked = jnp.where(live_rows > 0.0, out_cotangent[0], 0.0)
    mixed_grad = jnp.einsum(
        "ld,ed->le", cot_masked, output_proj, preferred_element_type=jnp.float32
    )
    attention_grad = norm_back(mixed_grad * gate_u, attn_normed, attn_spread).astype(jnp.bfloat16)

    def query_tile(running, pieces_blk, key_start):
        keys_blk, values_blk = pieces_blk
        key_pos = key_start + jnp.arange(keys_blk.shape[0], dtype=jnp.int32)
        allowed = tile_mask(positions, key_pos, length_user)
        return running + tile_query_grad(
            queries_loc, attention_grad, keys_blk, values_blk, allowed, score_scale
        )

    query_grad = over_blocks(
        query_tile,
        zero_rows,
        (
            lax.all_gather(keys_loc, "seq", axis=0, tiled=True),
            lax.all_gather(values_loc, "seq", axis=0, tiled=True),
        ),
    )

    def key_tile(running, pieces_blk, query_start):
        query_piece, grad_piece = pieces_blk
        rows_in = query_piece.shape[0]
        query_pos = query_start + jnp.arange(rows_in, dtype=jnp.int32)
        allowed = tile_mask(query_pos, positions, length_user)
        key_part, value_part = tile_key_grad(
            query_piece, grad_piece, keys_loc, values_loc, allowed, score_scale
        )
        return (running[0] + key_part, running[1] + value_part)

    key_grad, value_grad = over_blocks(
        key_tile,
        (zero_rows, zero_rows),
        (
            lax.all_gather(queries_loc, "seq", axis=0, tiled=True),
            lax.all_gather(attention_grad, "seq", axis=0, tiled=True),
        ),
    )
    activated_grad = jnp.concatenate(
        [mixed_grad * attn_normed, value_grad, query_grad, key_grad], axis=1
    )
    pre_grad = (activated_grad * dsilu(pre_act)).astype(jnp.bfloat16)
    norm_grad = jnp.einsum("lf,df->ld", pre_grad, input_proj, preferred_element_type=jnp.float32)
    embed_grad = cot_masked.astype(jnp.float32) + norm_back(norm_grad, normed_exact, input_spread)
    outgoing = jnp.zeros((owners * capacity, model_width), jnp.float32).at[slot_of].set(embed_grad)
    arrived = lax.all_to_all(
        outgoing.reshape(owners, capacity, model_width).astype(jnp.bfloat16),
        ("table", "seq"),
        split_axis=0,
        concat_axis=0,
        tiled=True,
    ).astype(jnp.float32)
    arrived = arrived.reshape(owners * capacity, model_width)
    arrived = jnp.where((asked_rows >= 0)[:, None], arrived, 0.0)
    table_sum = (
        jnp.zeros((rows_dev, model_width), jnp.float32).at[jnp.maximum(asked_rows, 0)].add(arrived)
    )
    return (layer_out[None], table_sum.astype(jnp.bfloat16))


def solution(mesh):
    placed = (
        P("table", "seq"),
        P("table"),
        P(),
        P(("table", "seq"), None),
        P(),
        P(),
        P("table", "seq", None),
    )
    return jax.shard_map(
        local,
        mesh=mesh,
        in_specs=placed,
        out_specs=(P("table", "seq", None), P(("table", "seq"), None)),
        check_vma=False,
    )
```

profile of v0, /device:TPU:1, one launch (start us, length us, event | category | flops | bytes accessed | tf_op | source)
XLA Modules:
  0.0 639.1 jit_solution(17129103487321654110)
XLA Ops:
  8.0 3.5 gather_fusion
  13.7 21.1 %all_to_all.19 = s32[128,1,6]{2,1,0:T(1,128)S(1)} all-to-all(s32[128,1,6]{2,1,0:T(1,128)S(1)} %bitcast.235), channel_id=1, replica_groups=mesh['table'=8,'seq'=16] {'table','seq'}, dimensions={0} | all-to-all | bytes 6144 | tf_op jit(solution)/shard_map/all_to_all | solution.py:145
  36.3 5.4 gather_fusion.1
  45.5 5.2 all-to-all-start.1
  50.8 19.0 %all-to-all-done.1 = bf16[128,6,512]{2,1,0:T(8,128)(2,1)} async-done(((bf16[128,6,512]{2,1,0:T(8,128)(2,1)}), bf16[128,6,512]{2,1,0:T(8,128)(2,1)}, u32[]{:S(2)}, u32[]{:S(2)}) %all-to-all-start.1) | async-done | bytes 786464 | tf_op jit(solution)/shard_map/all_to_all | solution.py:153
  83.4 40.5 %all-gather.5.cloned.1.call-done = bf16[4096,512]{1,0:T(8,128)(2,1)} async-done(((bf16[256,512]{1,0:T(8,128)(2,1)}), bf16[4096,512]{1,0:T(8,128)(2,1)}) %all-gather.5.cloned.1.call-update) | async-done | bytes 4194320 | tf_op jit(solution)/shard_map/all_gather | solution.py:186
  124.0 6.4 %copy.71 = bf16[8,512,512]{1,2,0:T(8,128)(2,1)} copy(bf16[8,512,512]{2,1,0:T(8,128)(2,1)} %bitcast.227) | data formatting | bytes 8388608
  130.4 47.0 %all-gather.7.cloned.1.call-done = bf16[4096,512]{1,0:T(8,128)(2,1)} async-done(((bf16[256,512]{1,0:T(8,128)(2,1)}), bf16[4096,512]{1,0:T(8,128)(2,1)}) %all-gather.7.cloned.1.call-update) | async-done | bytes 4194320 | tf_op jit(solution)/shard_map/all_gather | solution.py:185
  177.4 6.5 %copy.72 = bf16[8,512,512]{1,2,0:T(8,128)(2,1)} copy(bf16[8,512,512]{2,1,0:T(8,128)(2,1)} %bitcast.228) | data formatting | bytes 8388608
  183.8 79.6 %while.35 = (s32[]{:T(128)}, f32[256,512]{0,1:T(8,128)S(1)}, bf16[8,512,512]{1,2,0:T(8,128)(2,1)}, s32[8]{0:T(128)}, s32[]{:T(128)}, /*index=5*/bf16[8,512,512]{...) while((s32[]{:T(128)}, f32[256,512]{0,1:T(8,128)S(1)}, ...), condition=%wide.region_7.8_spmd.clone, body=%wide.region_6.7_spmd.clone.sunk | while | flops 276301056 | bytes 5773967 | solution.py:118
  188.8 3.9 fusion.128
  198.8 3.8 fusion.128
  208.7 3.8 fusion.128
  218.6 3.8 fusion.128
  228.6 3.8 fusion.128
  238.6 3.8 fusion.128
  248.5 3.8 fusion.128
  258.4 3.8 fusion.128
  270.8 120.8 %while.37 = (s32[]{:T(128)}, f32[256,512]{0,1:T(8,128)S(1)}, bf16[8,512,512]{1,2,0:T(8,128)(2,1)}, s32[8]{0:T(128)}, s32[]{:T(128)}, /*index=5*/bf16[8,512,512]{...) while((s32[]{:T(128)}, f32[256,512]{0,1:T(8,128)S(1)}, ...), condition=%wide.region_15.16_spmd.clone, body=%wide.region_14.15_spmd.clone.sunk | while | flops 414844160 | bytes 14949015 | solution.py:118
  275.6 3.6 fusion.143
  279.2 5.6 fusion.144
  290.8 3.6 fusion.143
  294.4 5.5 fusion.144
  305.9 3.6 fusion.143
  309.5 5.6 fusion.144
  321.1 3.6 fusion.143
  324.7 5.5 fusion.144
  336.1 3.6 fusion.143
  339.8 5.4 fusion.144
  351.2 3.6 fusion.143
  354.8 5.5 fusion.144
  366.3 3.6 fusion.143
  369.9 5.4 fusion.144
  381.3 3.6 fusion.143
  384.9 5.4 fusion.144
  392.6 177.3 %while.36 = (s32[]{:T(128)}, f32[256,512]{0,1:T(8,128)}, f32[256,512]{0,1:T(8,128)}, bf16[8,512,512]{2,1,0:T(8,128)(2,1)}, s32[8]{0:T(128)}, /*index=5*/s32[]{:T...) while((s32[]{:T(128)}, f32[256,512]{0,1:T(8,128)}, ...), condition=%wide.region_13.14_spmd.clone, body=%wide.region_12.13_spmd.clone.sunk | while | flops 556664576 | bytes 32382224 | solution.py:118
  402.4 5.5 fusion.137
  407.9 4.6 fusion.136
  419.7 2.8 fusion.135
  424.5 5.5 fusion.137
  430.0 4.6 fusion.136
  441.8 2.8 fusion.135
  446.7 5.5 fusion.137
  452.1 4.6 fusion.136
  468.8 5.5 fusion.137
  474.3 4.6 fusion.136
  486.1 2.8 fusion.135
  491.0 5.5 fusion.137
  496.4 4.6 fusion.136
  508.2 2.8 fusion.135
  513.1 5.5 fusion.137
  518.6 4.6 fusion.136
  530.4 2.8 fusion.135
  535.2 5.5 fusion.137
  540.7 4.6 fusion.136
  552.5 2.8 fusion.135
  557.4 5.5 fusion.137
  562.8 4.6 fusion.136
  572.5 3.8 fusion.80
  576.4 3.5 scatter_custom_fusion.1
  584.4 8.1 %all-to-all-start.2 = ((bf16[128,6,512]{2,1,0:T(8,128)(2,1)}), bf16[128,6,512]{2,1,0:T(8,128)(2,1)}, u32[]{:S(2)}, u32[]{:S(2)}) async-start(bf16[128,6,512]{2,1,0:T(8,128)(2,1)} %convert_element_type.79), calls=%async_computation.2 | async-start | bytes 2097152 | tf_op jit(solution)/shard_map/all_to_all | solution.py:241
  595.0 16.4 %all-to-all-done.2 = bf16[128,6,512]{2,1,0:T(8,128)(2,1)} async-done(((bf16[128,6,512]{2,1,0:T(8,128)(2,1)}), bf16[128,6,512]{2,1,0:T(8,128)(2,1)}, u32[]{:S(2)}, u32[]{:S(2)}) %all-to-all-start.2) | async-done | bytes 786464 | tf_op jit(solution)/shard_map/all_to_all | solution.py:241
  613.8 12.8 %scatter_custom_fusion.2 = f32[4096,512]{1,0:T(8,128)} fusion(s32[768]{0:T(1024)} %copy-done.12, f32[]{:T(128)} %constant.119.clone.1, f32[768,512]{1,0:T(8,128)} %reshape.445, pred[768]{0:T(1024)(128)(4,1)S(1)} %ge.20), kind=kCustom, calls=%fused_computation.69 | custom fusion | flops 786432 | bytes 9963264 | tf_op jit(solution)/shard_map/scatter-add | solution.py:251
  626.6 5.9 convert_element_type.80
  (367 shorter events, 217.1 us)
Async XLA Ops:
  7.2 65.6 %copy-start = (bf16[512,2048]{1,0:T(8,128)(2,1)S(1)}, bf16[512,2048]{1,0:T(8,128)(2,1)}, u32[]{:S(2)}) copy-start(bf16[512,2048]{1,0:T(8,128)(2,1)} %param.17) | copy-start | bytes 6291460
  12.1 38.7 %copy-start.17 = (s32[256,1]{0,1:T(1,128)}, s32[256,1]{0,1:T(1,128)S(1)}, u32[]{:S(2)}) copy-start(s32[256,1]{0,1:T(1,128)S(1)} %compare_select_fusion) | copy-start | bytes 3076
  34.8 0.6 copy-start.10
  35.7 0.6 copy-start.12
  45.5 24.3 %all-to-all-start.1 = ((bf16[128,6,512]{2,1,0:T(8,128)(2,1)}), bf16[128,6,512]{2,1,0:T(8,128)(2,1)}, u32[]{:S(2)}, u32[]{:S(2)}) async-start(bf16[128,6,512]{2,1,0:T(8,128)(2,1)} %broadcast_select_fusion), calls=%async_computation.1 | async-start | bytes 2097152 | tf_op jit(solution)/shard_map/all_to_all | solution.py:153
  50.8 73.2 %all-gather.5.cloned.1.call-start = ((), (), s32[]{:S(2)}) async-start(), calls=%async_computation.3 | async-start | bytes 4456448 | tf_op jit(solution)/shard_map/all_gather | solution.py:186
  72.4 3.2 copy-start.7
  72.5 3.0 copy-start.13
  72.8 2.8 copy-start.15
  76.5 100.9 %all-gather.7.cloned.1.call-start = ((), (), s32[]{:S(2)}) async-start(), calls=%async_computation.4 | async-start | bytes 4456448 | tf_op jit(solution)/shard_map/all_gather | solution.py:185
  77.2 315.4 %all-gather.9.cloned.1.call-start = ((), (), s32[]{:S(2)}) async-start(), calls=%async_computation.5 | async-start | bytes 4456448 | tf_op jit(solution)/shard_map/all_gather | solution.py:230
  78.5 187.4 %copy-start.18 = (pred[256]{0:T(512)(128)(4,1)}, pred[256]{0:T(512)(128)(4,1)S(1)}, u32[]{:S(2)}) copy-start(pred[256]{0:T(512)(128)(4,1)S(1)} %broadcast_compare_fusion.4) | copy-start | bytes 772
  83.2 309.4 %all-gather.11.cloned.1.call-start = ((), (), s32[]{:S(2)}) async-start(), calls=%async_computation.6 | async-start | bytes 4456448 | tf_op jit(solution)/shard_map/all_gather | solution.py:231
  264.5 3.3 copy-start.5
  269.9 0.9 copy-start.9
  392.6 179.8 %copy-start.14 = (f32[256]{0:T(256)S(1)}, f32[256]{0:T(256)}, u32[]{:S(2)}) copy-start(f32[256]{0:T(256)} %copy-done.13) | copy-start | bytes 3076
  392.6 179.9 %copy-start.16 = (f32[256]{0:T(256)S(1)}, f32[256]{0:T(256)}, u32[]{:S(2)}) copy-start(f32[256]{0:T(256)} %copy-done.15) | copy-start | bytes 3076
  407.9 4.6 copy-start.1
  407.9 4.6 copy-start.3
  414.0 0.8 copy-start.2
  414.0 1.0 copy-start.4
  430.0 4.6 copy-start.1
  430.0 4.6 copy-start.3
  436.1 0.8 copy-start.2
  436.2 1.0 copy-start.4
  452.1 4.6 copy-start.1
  452.1 4.6 copy-start.3
  458.3 0.8 copy-start.2
  458.3 1.0 copy-start.4
  474.3 4.6 copy-start.1
  474.3 4.6 copy-start.3
  480.4 0.8 copy-start.2
  480.4 1.0 copy-start.4
  496.4 4.6 copy-start.1
  496.4 4.6 copy-start.3
  502.6 0.8 copy-start.2
  502.6 1.0 copy-start.4
  518.6 4.6 copy-start.1
  518.6 4.6 copy-start.3
  524.7 0.8 copy-start.2
  524.7 1.0 copy-start.4
  540.7 4.6 copy-start.1
  540.7 4.6 copy-start.3
  546.8 0.8 copy-start.2
  546.8 1.0 copy-start.4
  562.8 4.6 copy-start.1
  562.8 4.6 copy-start.3
  569.0 0.8 copy-start.2
  569.0 1.0 copy-start.4
  572.5 3.8 copy-start.8
  572.5 3.8 copy-start.19
  576.3 16.2 %copy-start.11 = (s32[128,1,6]{0,2,1:T(8,128)S(1)}, s32[128,1,6]{0,2,1:T(8,128)}, u32[]{:S(2)}) copy-start(s32[128,1,6]{0,2,1:T(8,128)} %copy-done.10) | copy-start | bytes 9220
  576.3 16.5 %copy-start.6 = (f32[256,512]{1,0:T(8,128)S(1)}, f32[256,512]{1,0:T(8,128)}, u32[]{:S(2)}) copy-start(f32[256,512]{1,0:T(8,128)} %copy.74) | copy-start | bytes 1572868
  579.8 13.0 %copy-start.20 = (bf16[512,512]{1,0:T(8,128)(2,1)S(1)}, bf16[512,512]{1,0:T(8,128)(2,1)}, u32[]{:S(2)}) copy-start(bf16[512,512]{1,0:T(8,128)(2,1)} %param.18) | copy-start | bytes 1572868
  584.4 27.0 %all-to-all-start.2 = ((bf16[128,6,512]{2,1,0:T(8,128)(2,1)}), bf16[128,6,512]{2,1,0:T(8,128)(2,1)}, u32[]{:S(2)}, u32[]{:S(2)}) async-start(bf16[128,6,512]{2,1,0:T(8,128)(2,1)} %convert_element_type.79), calls=%async_computation.2 | async-start | bytes 2097152 | tf_op jit(solution)/shard_map/all_to_all | solution.py:241
Sparse Core Ops, SparseCore 0:
  76.6 47.3 all-gather.4
  126.1 51.2 all-gather.6
  179.5 51.2 all-gather.8
  270.9 51.2 all-gather.10
where the time goes:
time: 644 us; the launch traced here: 639 us
  matrix products  216 us (34%)
  local copies, waits for them, and re-layouts  143 us (22%)
  waiting for transfers between devices  124 us (19%)
  other arithmetic  104 us (16%)
  blocking collectives  21.1 us (3%)
  between operations  14.9 us (2%)
  starting transfers between devices  13.7 us (2%)
    dynamic_slice x72, local copies, waits for them, and re-layouts, over_blocks(): result, unused = lax.scan(step_block, running, (offsets, stacked))  90.7 us
    all_gather x1, waiting for transfers between devices, local(): lax.all_gather(keys_loc, 'seq', axis=0, tiled=True)  47 us
    dot_general x8, matrix products, tile_query_grad(): jnp.einsum('hln,nhe->lhe', score_grad, heads_view(keys_blk), preferred_el...  43.9 us
    dot_general x8, matrix products, tile_key_grad(): jnp.einsum('hln,lhe->nhe', score_grad, heads_view(query_piece), preferred...  43.6 us
    all_gather x1, waiting for transfers between devices, local(): lax.all_gather(values_loc, 'seq', axis=0, tiled=True)  40.5 us
    dot_general x8, matrix products, tile_key_grad(): jnp.einsum('hln,lhe->nhe', weights, heads_view(grad_piece), preferred_ele...  36.6 us
    dot_general x8, matrix products, tile_forward(): jnp.einsum('hln,nhe->lhe', weights, heads_view(values_blk), preferred_ele...  30.6 us
    dot_general x8, matrix products, tile_query_grad(): jnp.einsum('lhe,nhe->hln', heads_view(queries), heads_view(keys_blk), pre...  29.1 us
  transfers between devices with their start and end apart: 6, of which 4 were waited for; matrix products, arithmetic and copies ran while one was open for 36% of the time, Pallas kernels for 0%

commit v1 on v0

--- a/solution.py
+++ b/solution.py
@@ -182,7 +182,9 @@
         forward_tile,
         zero_rows,
         (
-            lax.all_gather(keys_loc, "seq", axis=0, tiled=True),
+            jnp.concatenate(
+                lax.all_to_all(jnp.stack([keys_loc] * lax.axis_size("seq")), "seq", 0, 0), axis=0
+            ),
             lax.all_gather(values_loc, "seq", axis=0, tiled=True),
         ),
     )

time: 644 us -> 651 us (1.011)
  local copies, waits for them, and re-layouts: 143 us -> 169 us
  other arithmetic: 104 us -> 95.4 us
  waiting for transfers between devices: 124 us -> 117 us
    all_gather x1, waiting for transfers between devices: 47 us -> 0.02 us  [local(): lax.all_gather(keys_loc, 'seq', axis=0, tiled=True)]
    all_gather x1, waiting for transfers between devices: 40.5 us -> 80.5 us  [local(): lax.all_gather(values_loc, 'seq', axis=0, tiled=True)]
    dynamic_slice x72 -> x104, local copies, waits for them, and re-layouts: 90.7 us -> 115 us  [over_blocks(): result, unused = lax.scan(step_block, running, (offsets, stacked))]
    unnamed x41 -> x46, local copies, waits for them, and re-layouts: 19.7 us -> 10.4 us
    add x8, other arithmetic: 9.44 us -> 0.98 us  [forward_tile(): running + tile_forward(queries_loc, keys_blk, values_blk, allowed, score_...]
    while x64 -> x96, local copies, waits for them, and re-layouts: 7.91 us -> 14.7 us
  transfers between devices with their start and end apart: 6 -> 7, of which waited for: 4 -> 3; matrix products, arithmetic and copies ran while one was open for 36% -> 36% of each run, Pallas kernels for 0% -> 0%
where the time goes in v1:
time: 651 us; the launch traced here: 645 us
  matrix products  210 us (32%)
  local copies, waits for them, and re-layouts  169 us (26%)
  waiting for transfers between devices  117 us (18%)
  other arithmetic  95.4 us (15%)
  blocking collectives  21.1 us (3%)
  starting transfers between devices  16.3 us (3%)
  between operations  14.9 us (2%)
    dynamic_slice x104, local copies, waits for them, and re-layouts, over_blocks(): result, unused = lax.scan(step_block, running, (offsets, stacked))  115 us
    all_gather x1, waiting for transfers between devices, local(): lax.all_gather(values_loc, 'seq', axis=0, tiled=True)  80.5 us
    dot_general x8, matrix products, tile_query_grad(): jnp.einsum('hln,nhe->lhe', score_grad, heads_view(keys_blk), preferred_el...  44.6 us
    dot_general x8, matrix products, tile_key_grad(): jnp.einsum('hln,lhe->nhe', score_grad, heads_view(query_piece), preferred...  43.7 us
    dot_general x8, matrix products, tile_key_grad(): jnp.einsum('hln,lhe->nhe', weights, heads_view(grad_piece), preferred_ele...  36.2 us
    dot_general x8, matrix products, tile_query_grad(): jnp.einsum('lhe,nhe->hln', heads_view(queries), heads_view(keys_blk), pre...  29 us
    dot_general x8, matrix products, tile_forward(): jnp.einsum('hln,nhe->lhe', weights, heads_view(values_blk), preferred_ele...  24.2 us
    dot_general x8, matrix products, tile_key_grad(): jnp.einsum('lhe,nhe->hln', heads_view(query_piece), heads_view(keys_mine)...  22.2 us
  transfers between devices with their start and end apart: 7, of which 3 were waited for; matrix products, arithmetic and copies ran while one was open for 36% of the time, Pallas kernels for 0%

profile of v1, /device:TPU:1, one launch (start us, length us, event | category | flops | bytes accessed | tf_op | source)
XLA Modules:
  0.0 645.4 jit_solution(8881724493695512591)
XLA Ops:
  8.0 3.5 gather_fusion
  13.7 21.1 %all_to_all.24 = s32[128,1,6]{2,1,0:T(1,128)S(1)} all-to-all(s32[128,1,6]{2,1,0:T(1,128)S(1)} %bitcast.236), channel_id=1, replica_groups=mesh['table'=8,'seq'=16] {'table','seq'}, dimensions={0} | all-to-all | bytes 6144 | tf_op jit(solution)/shard_map/all_to_all | solution.py:145
  36.3 5.4 gather_fusion.1
  45.5 5.2 all-to-all-start.1
  50.8 19.0 %all-to-all-done.1 = bf16[128,6,512]{2,1,0:T(8,128)(2,1)} async-done(((bf16[128,6,512]{2,1,0:T(8,128)(2,1)}), bf16[128,6,512]{2,1,0:T(8,128)(2,1)}, u32[]{:S(2)}, u32[]{:S(2)}) %all-to-all-start.1) | async-done | bytes 786464 | tf_op jit(solution)/shard_map/all_to_all | solution.py:153
  72.8 2.8 fusion.81
  77.2 3.3 stack.2
  80.5 4.7 all-to-all-start.2
  88.7 80.5 %all-gather.5.cloned.1.call-done = bf16[4096,512]{1,0:T(8,128)(2,1)} async-done(((bf16[256,512]{1,0:T(8,128)(2,1)}), bf16[4096,512]{1,0:T(8,128)(2,1)}) %all-gather.5.cloned.1.call-update) | async-done | bytes 4194320 | tf_op jit(solution)/shard_map/all_gather | solution.py:188
  169.2 6.4 copy.70
  175.6 80.5 %while.35 = (s32[]{:T(128)}, f32[256,512]{0,1:T(8,128)S(1)}, bf16[8,512,512]{1,2,0:T(8,128)(2,1)}, s32[8]{0:T(128)}, s32[]{:T(128)}, /*index=5*/bf16[8,512,512]{...) while((s32[]{:T(128)}, f32[256,512]{0,1:T(8,128)S(1)}, ...), condition=%wide.region_7.8_spmd.clone, body=%wide.region_6.7_spmd.clone.sunk | while | flops 276301056 | bytes 6822547 | solution.py:118
  182.5 3.0 fusion.128
  192.5 3.0 fusion.128
  202.5 3.0 fusion.128
  212.6 3.0 fusion.128
  222.6 3.0 fusion.128
  232.7 3.0 fusion.128
  242.7 3.0 fusion.128
  252.7 3.2 fusion.128
  261.4 136.9 %while.37 = (s32[]{:T(128)}, f32[256,512]{0,1:T(8,128)}, bf16[8,512,512]{2,1,0:T(8,128)(2,1)}, s32[8]{0:T(128)}, s32[]{:T(128)}, /*index=5*/bf16[8,512,512]{1,2,...) while((s32[]{:T(128)}, f32[256,512]{0,1:T(8,128)}, ...), condition=%wide.region_15.16_spmd.clone, body=%wide.region_14.15_spmd.clone.sunk | while | flops 414844160 | bytes 20191956 | solution.py:118
  265.5 3.6 fusion.143
  271.0 5.5 fusion.144
  282.5 3.6 fusion.143
  288.0 5.5 fusion.144
  299.6 3.6 fusion.143
  305.1 5.9 fusion.144
  317.0 3.6 fusion.143
  322.6 5.5 fusion.144
  334.1 3.6 fusion.143
  339.6 5.5 fusion.144
  351.2 3.6 fusion.143
  356.7 5.5 fusion.144
  368.2 3.6 fusion.143
  373.7 5.5 fusion.144
  385.3 3.6 fusion.143
  390.8 5.5 fusion.144
  400.4 178.0 %while.36 = (s32[]{:T(128)}, f32[256,512]{0,1:T(8,128)}, f32[256,512]{0,1:T(8,128)}, bf16[8,512,512]{2,1,0:T(8,128)(2,1)}, s32[8]{0:T(128)}, /*index=5*/s32[]{:T...) while((s32[]{:T(128)}, f32[256,512]{0,1:T(8,128)}, ...), condition=%wide.region_13.14_spmd.clone, body=%wide.region_12.13_spmd.clone.sunk | while | flops 556664576 | bytes 32382224 | solution.py:118
  405.3 2.8 fusion.135
  410.2 5.5 fusion.137
  415.7 4.5 fusion.136
  432.4 5.5 fusion.137
  437.9 4.5 fusion.136
  449.8 2.8 fusion.135
  454.7 5.5 fusion.137
  460.1 4.5 fusion.136
  472.0 2.8 fusion.135
  476.9 5.5 fusion.137
  482.3 4.5 fusion.136
  494.2 2.8 fusion.135
  499.1 5.5 fusion.137
  504.6 4.5 fusion.136
  521.3 5.5 fusion.137
  526.8 4.5 fusion.136
  538.6 2.8 fusion.135
  543.5 5.5 fusion.137
  549.0 4.5 fusion.136
  565.7 5.5 fusion.137
  571.2 4.5 fusion.136
  580.9 3.8 fusion.80
  584.7 3.5 scatter_custom_fusion.1
  592.8 6.1 all-to-all-start.3
  601.3 16.5 %all-to-all-done.3 = bf16[128,6,512]{2,1,0:T(8,128)(2,1)} async-done(((bf16[128,6,512]{2,1,0:T(8,128)(2,1)}), bf16[128,6,512]{2,1,0:T(8,128)(2,1)}, u32[]{:S(2)}, u32[]{:S(2)}) %all-to-all-start.3) | async-done | bytes 786464 | tf_op jit(solution)/shard_map/all_to_all | solution.py:243
  620.1 12.8 %scatter_custom_fusion.2 = f32[4096,512]{1,0:T(8,128)} fusion(s32[768]{0:T(1024)} %copy-done.17, f32[]{:T(128)} %constant.119.clone.1, f32[768,512]{1,0:T(8,128)} %reshape.446, pred[768]{0:T(1024)(128)(4,1)S(1)} %ge.20), kind=kCustom, calls=%fused_computation.69 | custom fusion | flops 786432 | bytes 9963264 | tf_op jit(solution)/shard_map/scatter-add | solution.py:253
  632.9 5.9 convert_element_type.80
  (439 shorter events, 236.7 us)
Async XLA Ops:
  7.2 65.6 %copy-start = (bf16[512,2048]{1,0:T(8,128)(2,1)S(1)}, bf16[512,2048]{1,0:T(8,128)(2,1)}, u32[]{:S(2)}) copy-start(bf16[512,2048]{1,0:T(8,128)(2,1)} %param.17) | copy-start | bytes 6291460
  12.1 38.7 %copy-start.22 = (s32[256,1]{0,1:T(1,128)}, s32[256,1]{0,1:T(1,128)S(1)}, u32[]{:S(2)}) copy-start(s32[256,1]{0,1:T(1,128)S(1)} %compare_select_fusion) | copy-start | bytes 3076
  45.5 24.3 %all-to-all-start.1 = ((bf16[128,6,512]{2,1,0:T(8,128)(2,1)}), bf16[128,6,512]{2,1,0:T(8,128)(2,1)}, u32[]{:S(2)}, u32[]{:S(2)}) async-start(bf16[128,6,512]{2,1,0:T(8,128)(2,1)} %broadcast_select_fusion), calls=%async_computation.1 | async-start | bytes 2097152 | tf_op jit(solution)/shard_map/all_to_all | solution.py:153
  50.8 118.4 %all-gather.5.cloned.1.call-start = ((), (), s32[]{:S(2)}) async-start(), calls=%async_computation.4 | async-start | bytes 4456448 | tf_op jit(solution)/shard_map/all_gather | solution.py:188
  72.4 3.2 copy-start.10
  72.5 3.1 copy-start.18
  72.8 2.8 copy-start.20
  76.5 11.1 %copy-start.13 = (bf16[256,512]{1,0:T(8,128)(2,1)}, bf16[256,512]{1,0:T(8,128)(2,1)S(1)}, u32[]{:S(2)}) copy-start(bf16[256,512]{1,0:T(8,128)(2,1)S(1)} %get-tuple-element.419) | copy-start | bytes 786436
  76.5 184.9 %all-gather.11.cloned.1.call-start = ((), (), s32[]{:S(2)}) async-start(), calls=%async_computation.7 | async-start | bytes 4456448 | tf_op jit(solution)/shard_map/all_gather | solution.py:213
  80.5 6.0 copy-start.14
  80.5 6.9 %copy-start.9 = (bf16[256,512]{1,0:T(8,128)(2,1)S(1)}, bf16[256,512]{1,0:T(8,128)(2,1)}, u32[]{:S(2)}) copy-start(bf16[256,512]{1,0:T(8,128)(2,1)} %get-tuple-element.420) | copy-start | bytes 786436
  80.5 95.1 %all-to-all-start.2 = ((bf16[16,256,512]{2,1,0:T(8,128)(2,1)}), bf16[16,256,512]{2,1,0:T(8,128)(2,1)}, u32[]{:S(2)}, u32[]{:S(2)}) async-start(bf16[16,256,512]{2,1,0:T(8,128)(2,1)} %stack.2), calls=%async_computation.2 | async-start | bytes 8388608 | tf_op jit(solution)/shard_map/all_to_all | solution.py:186
  85.2 315.1 %all-gather.7.cloned.1.call-start = ((), (), s32[]{:S(2)}) async-start(), calls=%async_computation.5 | async-start | bytes 4456448 | tf_op jit(solution)/shard_map/all_gather | solution.py:232
  86.5 170.1 %copy-start.23 = (pred[256]{0:T(512)(128)(4,1)}, pred[256]{0:T(512)(128)(4,1)S(1)}, u32[]{:S(2)}) copy-start(pred[256]{0:T(512)(128)(4,1)S(1)} %broadcast_compare_fusion.4) | copy-start | bytes 772
  88.4 311.9 %all-gather.9.cloned.1.call-start = ((), (), s32[]{:S(2)}) async-start(), calls=%async_computation.6 | async-start | bytes 4456448 | tf_op jit(solution)/shard_map/all_gather | solution.py:233
  256.3 5.1 copy-start.7
  260.5 0.9 copy-start.12
  271.0 5.5 copy-start.1
  288.0 5.5 copy-start.1
  305.1 5.9 copy-start.1
  322.6 5.5 copy-start.1
  339.6 5.5 copy-start.1
  356.7 5.5 copy-start.1
  373.7 5.5 copy-start.1
  390.8 5.5 copy-start.1
  400.4 180.5 %copy-start.19 = (f32[256]{0:T(256)S(1)}, f32[256]{0:T(256)}, u32[]{:S(2)}) copy-start(f32[256]{0:T(256)} %copy-done.18) | copy-start | bytes 3076
  400.4 180.5 %copy-start.21 = (f32[256]{0:T(256)S(1)}, f32[256]{0:T(256)}, u32[]{:S(2)}) copy-start(f32[256]{0:T(256)} %copy-done.20) | copy-start | bytes 3076
  415.7 4.5 copy-start.3
  415.7 4.5 copy-start.5
  421.8 0.8 copy-start.4
  421.8 1.1 copy-start.6
  437.9 4.5 copy-start.3
  437.9 4.5 copy-start.5
  444.0 0.8 copy-start.4
  444.0 1.1 copy-start.6
  460.1 4.5 copy-start.3
  460.1 4.5 copy-start.5
  466.2 0.8 copy-start.4
  466.2 1.1 copy-start.6
  482.3 4.5 copy-start.3
  482.3 4.5 copy-start.5
  488.4 0.8 copy-start.4
  488.4 1.1 copy-start.6
  504.5 4.5 copy-start.3
  504.6 4.5 copy-start.5
  510.6 0.8 copy-start.4
  510.7 1.1 copy-start.6
  526.8 4.5 copy-start.3
  526.8 4.5 copy-start.5
  532.9 1.1 copy-start.6
  549.0 4.5 copy-start.3
  549.0 4.5 copy-start.5
  555.1 0.8 copy-start.4
  555.1 1.1 copy-start.6
  571.2 4.5 copy-start.3
  571.2 4.5 copy-start.5
  577.3 0.8 copy-start.4
  577.3 1.1 copy-start.6
  580.9 3.8 copy-start.11
  580.9 3.8 copy-start.24
  584.7 14.2 %copy-start.16 = (s32[128,1,6]{0,2,1:T(8,128)S(1)}, s32[128,1,6]{0,2,1:T(8,128)}, u32[]{:S(2)}) copy-start(s32[128,1,6]{0,2,1:T(8,128)} %copy-done.15) | copy-start | bytes 9220
  584.7 14.5 %copy-start.8 = (f32[256,512]{1,0:T(8,128)S(1)}, f32[256,512]{1,0:T(8,128)}, u32[]{:S(2)}) copy-start(f32[256,512]{1,0:T(8,128)} %copy-done.7) | copy-start | bytes 1572868
  588.2 11.0 %copy-start.25 = (bf16[512,512]{1,0:T(8,128)(2,1)S(1)}, bf16[512,512]{1,0:T(8,128)(2,1)}, u32[]{:S(2)}) copy-start(bf16[512,512]{1,0:T(8,128)(2,1)} %param.18) | copy-start | bytes 1572868
  592.8 25.0 %all-to-all-start.3 = ((bf16[128,6,512]{2,1,0:T(8,128)(2,1)}), bf16[128,6,512]{2,1,0:T(8,128)(2,1)}, u32[]{:S(2)}, u32[]{:S(2)}) async-start(bf16[128,6,512]{2,1,0:T(8,128)(2,1)} %convert_element_type.79), calls=%async_computation.3 | async-start | bytes 2097152 | tf_op jit(solution)/shard_map/all_to_all | solution.py:243
  (11 other events, 8.4 us)
Sparse Core Ops, SparseCore 0:
  76.6 92.5 all-gather.4
  171.3 48.8 all-gather.10
  222.3 51.2 all-gather.6
  275.6 51.2 all-gather.8
